TPU v7x, 128 devices: a whole 4x4x4 slice. The times are simulated.
128 devices in a mesh: seq: 32 (over x, y, core), head: 4 (over z).
Axes of the slice: x: 4, y: 4, z: 4, core: 2. Of those that a mesh axis runs over, the one named last changes fastest.
Arguments:
- query_rows: bfloat16 [16384, 64, 128], P('seq', 'head'), may hold values from -3 to 3
- key_rows: bfloat16 [16384, 64, 128], P('seq', 'head'), may hold values from -0.59765625 to 0.59765625
- value_rows: bfloat16 [16384, 64, 128], P('seq', 'head'), may hold values from -18 to 18
- output_grad: bfloat16 [16384, 64, 128], P('seq', 'head'), may hold values from -1.796875 to 1.796875
- norm_gain: float32 [64, 128], P('head'), may hold values from 0.1 to 1.9
- log_decay: float32 [64, 16384], P('head', 'seq'), may hold values from -0.6932 to 0, as said below
Outputs:
- normed: bfloat16 [16384, 64, 128], P('seq', 'head')
- grad_q: bfloat16 [16384, 64, 128], P('seq', 'head')
- grad_k: bfloat16 [16384, 64, 128], P('seq', 'head')
- grad_v: bfloat16 [16384, 64, 128], P('seq', 'head')
Inputs may be any that keep to these rules, and one draw needn't show every extreme that they name: `log_decay`: never positive.
All inputs are finite; a program needn't handle non-finite values.
Results may differ from a plain program's by a relative error of at most 0.0051.
Values sent between devices are 32-bit elements; how exact they have to be, the bound alone decides.
A program may use at most 192 MiB of HBM per device.

v0:
```python
import functools

import jax
import jax.numpy as jnp
from jax import lax
from jax.experimental import pallas as pl
from jax.experimental.pallas import tpu as pltpu
from jax.sharding import PartitionSpec as P

HEAD_TOTAL = 64
HD = 128
BLOCK = 256
CHUNK = 64
PAD = 8
MESH = pl.DeviceIdType.MESH
F32 = jnp.float32
BF16 = jnp.bfloat16


def dot(a, b, ca, cb):
    return lax.dot_general(a, b, (((ca,), (cb,)), ((), ())), preferred_element_type=F32)


def split(x, axis):
    hi = x.astype(BF16)
    lo = (x - hi.astype(F32)).astype(BF16)
    return jnp.concatenate([hi, lo], axis=axis)


def twice(x):
    return jnp.concatenate([x, x], axis=1)


def kernel(
    chips,
    q_hbm,
    k_hbm,
    v_hbm,
    g_hbm,
    gain_ref,
    ld_ref,
    normed_hbm,
    gq_hbm,
    gk_hbm,
    gv_hbm,
    land,
    hm,
    cumr,
    colc,
    att,
    wts,
    gkp,
    gvp,
    s0,
    g1,
    ob,
    gains,
    tx,
    tp,
    tm,
    sb,
    rb,
    pb,
    pin,
    es,
    ee,
    zb,
    sqacc,
    pracc,
    in_sem,
    out_sem,
    p1s,
    p1r,
    a1s,
    a1r,
    a2s,
    a2r,
    p2s,
    p2r,
    zs,
    zr,
):
    heads, tok = ld_ref.shape
    half = heads // 2
    nblocks = tok // BLOCK
    zcount = HEAD_TOTAL // heads
    d = lax.axis_index("seq")
    z = lax.axis_index("head")
    c = d // 2
    core = d - 2 * c
    partner = (2 * c + 1 - core, z)
    KS, VS, QS, GS = 0, 1, 2, 3

    def chip_dev(chip):
        return (2 * chip + core, z)

    def load(slot, src):
        return pltpu.make_async_copy(src, land.at[slot], in_sem.at[slot])

    sources = (k_hbm, v_hbm, q_hbm, g_hbm)
    for slot in range(4):
        load(slot, sources[slot]).start()

    barrier = pltpu.get_barrier_semaphore()

    def greet(i, _):
        pl.semaphore_signal(
            barrier, inc=1, device_id=chip_dev(lax.rem(c + i, chips)), device_id_type=MESH
        )
        return 0

    lax.fori_loop(1, chips, greet, 0)
    pl.semaphore_signal(barrier, inc=1, device_id=partner, device_id_type=MESH)
    for i in range(1, zcount):
        pl.semaphore_signal(
            barrier, inc=1, device_id=(d, lax.rem(z + i, zcount)), device_id_type=MESH
        )

    cum = ld_ref[...]
    lane = lax.broadcasted_iota(jnp.int32, cum.shape, 1) % BLOCK
    step = 1
    while step < BLOCK:
        cum = cum + jnp.where(lane >= step, pltpu.roll(cum, step, 1), 0.0)
        step *= 2
    for h in range(heads):
        cumr[h] = jnp.broadcast_to(cum[h : h + 1, :], (8, tok))
        gains[h] = jnp.broadcast_to(gain_ref[h : h + 1, :], (8, HD))

    def columns(h, _):
        colc[h] = jnp.transpose(jnp.broadcast_to(cumr[h, 0:1, :], (HD, tok)))
        return 0

    lax.fori_loop(0, heads, columns, 0)

    def to_heads(slot):
        load(slot, sources[slot]).wait()

        def part(i, _):
            at = pl.ds(pl.multiple_of(i * CHUNK, CHUNK), CHUNK)
            hm[slot, :, at, :] = pltpu.einshape("thd->htd", land[slot, at])
            return 0

        lax.fori_loop(0, tok // CHUNK, part, 0)

    def store_rows(slot, src, dst):
        def part(i, _):
            at = pl.ds(pl.multiple_of(i * CHUNK, CHUNK), CHUNK)
            land[slot, at] = pltpu.einshape("htd->thd", src[:, at, :])
            pltpu.make_async_copy(land.at[slot, at], dst.at[at], out_sem.at[slot, i]).start()
            return 0

        lax.fori_loop(0, tok // CHUNK, part, 0)

    def store_wait(slot, dst):
        def part(i, _):
            at = pl.ds(pl.multiple_of(i * CHUNK, CHUNK), CHUNK)
            pltpu.make_async_copy(land.at[slot, at], dst.at[at], out_sem.at[slot, i]).wait()
            return 0

        lax.fori_loop(0, tok // CHUNK, part, 0)

    def rows(b):
        return slice(b * BLOCK, (b + 1) * BLOCK)

    def end_row(h, b):
        return colc[h, (b + 1) * BLOCK - 1 : (b + 1) * BLOCK, :]

    mask = lax.broadcasted_iota(jnp.int32, (BLOCK, BLOCK), 0) >= lax.broadcasted_iota(
        jnp.int32, (BLOCK, BLOCK), 1
    )

    def decay_table(h, b):
        gap = twice(colc[h, rows(b), :]) - cumr[h, 0:1, rows(b)]
        return jnp.exp(jnp.where(mask, gap, -jnp.inf))

    def pair1(w, j):
        return pltpu.make_async_remote_copy(
            tx.at[w, j],
            tp.at[w, j],
            p1s.at[w, j],
            p1r.at[w, j],
            device_id=partner,
            device_id_type=MESH,
        )

    def spread1(w, dest, src):
        return pltpu.make_async_remote_copy(
            sb.at[w, dest],
            rb.at[w, src],
            a1s.at[w, dest],
            a1r.at[w, src],
            device_id=chip_dev(dest),
            device_id_type=MESH,
        )

    def spread2(w, dest, src):
        return pltpu.make_async_remote_copy(
            pb.at[w, dest],
            pin.at[w, src],
            a2s.at[w, dest],
            a2r.at[w, src],
            device_id=chip_dev(dest),
            device_id_type=MESH,
        )

    def pair2(w, j, owner):
        return pltpu.make_async_remote_copy(
            es.at[w, j],
            ee.at[w, owner * half + j],
            p2s.at[w, j],
            p2r.at[w, j],
            device_id=partner,
            device_id_type=MESH,
        )

    def begin(w, local_total):
        first = (core == 0) if w == 0 else (core == 1)

        def theirs(j, _):
            total, decay = local_total((1 - core) * half + j)
            tx[w, j, :HD] = total
            tx[w, j, HD:] = jnp.broadcast_to(decay, (PAD, HD))
            pair1(w, j).start()
            return 0

        lax.fori_loop(0, half, theirs, 0)

        def ours(i, _):
            j = lax.rem(i + c // 2, half)
            total, decay = local_total(core * half + j)
            tm[w, j, :HD] = total
            tm[w, j, HD:] = jnp.broadcast_to(decay, (PAD, HD))
            pair1(w, j).wait_recv()
            other = tp[w, j, :HD]
            other_decay = tp[w, j, HD : HD + 1]
            chip_total = jnp.where(first, other_decay, 1.0) * total + jnp.where(first, 1.0, decay) * other
            chip_decay = jnp.broadcast_to(decay * other_decay, (PAD, HD))
            for part in range(2):
                dest = 2 * j + part
                piece = chip_total[part * (HD // 2) : (part + 1) * (HD // 2)]
                sb[w, dest, : HD // 2] = piece
                sb[w, dest, HD // 2 :] = chip_decay

                @pl.when(dest != c)
                def _():
                    spread1(w, dest, c).start()

                @pl.when(dest == c)
                def _():
                    rb[w, c, : HD // 2] = piece
                    rb[w, c, HD // 2 :] = chip_decay

            return 0

        lax.fori_loop(0, half, ours, 0)

    def middle(w):
        def wait(i, _):
            src = lax.rem(c + i, chips)
            spread1(w, src, src).wait_recv()
            return 0

        lax.fori_loop(1, chips, wait, 0)
        carried = jnp.zeros((HD // 2, HD), F32)
        for i in range(chips):
            src = i if w == 0 else chips - 1 - i
            pb[w, src] = carried
            carried = rb[w, src, HD // 2 : HD // 2 + 1] * carried + rb[w, src, : HD // 2]

        def send(i, _):
            spread2(w, lax.rem(c + i, chips), c).start()
            return 0

        lax.fori_loop(1, chips, send, 0)
        pin[w, c] = pb[w, c]

    def finish(w, use):
        first = (core == 0) if w == 0 else (core == 1)

        def ours(i, _):
            j = lax.rem(i + c // 2, half)
            for part in range(2):
                src = 2 * j + part

                @pl.when(src != c)
                def _():
                    spread2(w, src, src).wait_recv()

            entering = jnp.concatenate([pin[w, 2 * j], pin[w, 2 * j + 1]], axis=0)
            decay = jnp.where(first, tm[w, j, HD : HD + 1], tp[w, j, HD : HD + 1])
            total = jnp.where(first, tm[w, j, :HD], tp[w, j, :HD])
            after = decay * entering + total
            es[w, j] = jnp.where(first, after, entering)
            pair2(w, j, core).start()
            ee[w, core * half + j] = jnp.where(first, entering, after)
            return 0

        lax.fori_loop(0, half, ours, 0)

        def use_ours(j, _):
            use(core * half + j)
            return 0

        lax.fori_loop(0, half, use_ours, 0)

        def use_theirs(i, _):
            j = lax.rem(i + c // 2, half)
            pair2(w, j, 1 - core).wait_recv()
            use((1 - core) * half + j)
            return 0

        lax.fori_loop(0, half, use_theirs, 0)

    def drain(w):
        def pairs(j, _):
            pair1(w, j).wait_send()
            pair2(w, j, core).wait_send()
            return 0

        lax.fori_loop(0, half, pairs, 0)

        def spreads(i, _):
            dest = lax.rem(c + i, chips)
            spread1(w, dest, c).wait_send()
            spread2(w, dest, c).wait_send()
            return 0

        lax.fori_loop(1, chips, spreads, 0)

    to_heads(KS)
    to_heads(VS)

    def key_value(h):
        parts = []
        for b in range(nblocks):
            scale = jnp.exp(end_row(h, b) - colc[h, rows(b), :])
            scaled = split(hm[VS, h, rows(b), :].astype(F32) * scale, 1)
            both = dot(hm[KS, h, rows(b), :], scaled, 0, 0)
            parts.append(both[:, :HD] + both[:, HD:])
        s0[h] = parts[0]
        return (
            jnp.exp(end_row(h, 1)) * parts[0] + parts[1],
            jnp.exp(end_row(h, 0) + end_row(h, 1)),
        )

    pl.semaphore_wait(barrier, chips - 1 + 1 + zcount - 1)
    begin(0, key_value)
    to_heads(QS)

    def intra_forward(h, _):
        for b in range(nblocks):
            raw = dot(hm[QS, h, rows(b), :], hm[KS, h, rows(b), :], 1, 1)
            weights = (raw * decay_table(h, b)).astype(BF16)
            wts[h, b] = weights
            att[h, rows(b), :] = dot(weights, hm[VS, h, rows(b), :], 1, 0)
        return 0

    lax.fori_loop(0, half, intra_forward, 0)
    middle(0)
    lax.fori_loop(half, heads, intra_forward, 0)
    to_heads(GS)

    def states(h):
        enter = ee[0, h]
        return enter, jnp.exp(end_row(h, 0)) * enter + s0[h]

    sqacc[...] = jnp.zeros_like(sqacc)
    pracc[...] = jnp.zeros_like(pracc)

    def attend(h):
        at_block = states(h)
        gain = gains[h, 0:1, :]
        for b in range(nblocks):
            carried = dot(twice(hm[QS, h, rows(b), :]), split(at_block[b], 0), 1, 0)
            whole = att[h, rows(b), :] + jnp.exp(colc[h, rows(b), :]) * carried
            att[h, rows(b), :] = whole
            sqacc[rows(b), :] += whole * whole
            pracc[rows(b), :] += (gain * hm[GS, h, rows(b), :].astype(F32)) * whole

    finish(0, attend)

    zb[0, 0:1, :] = jnp.sum(jnp.transpose(sqacc[...]), axis=0, keepdims=True)
    zb[0, 1:2, :] = jnp.sum(jnp.transpose(pracc[...]), axis=0, keepdims=True)
    zb[0, 2:, :] = jnp.zeros((6, tok), F32)

    def across(i):
        return pltpu.make_async_remote_copy(
            zb.at[0],
            zb.at[i],
            zs.at[i],
            zr.at[i],
            device_id=(d, lax.rem(z + i, zcount)),
            device_id_type=MESH,
        )

    for i in range(1, zcount):
        across(i).start()
    for i in range(1, zcount):
        across(i).wait()
    summed = zb[0]
    for i in range(1, zcount):
        summed = summed + zb[i]
    inv_row = lax.rsqrt(summed[0:1, :] / (HEAD_TOTAL * HD) + 1e-06)
    mean_row = summed[1:2, :] * inv_row / (HEAD_TOTAL * HD)
    sqacc[...] = jnp.transpose(jnp.broadcast_to(inv_row, (HD, tok)))
    pracc[...] = jnp.transpose(jnp.broadcast_to(inv_row * mean_row, (HD, tok)))

    def query_grad(h):
        gain = gains[h, 0:1, :]
        parts = []
        for b in range(nblocks):
            scaled = gain * hm[GS, h, rows(b), :].astype(F32)
            grad = ((scaled - att[h, rows(b), :] * pracc[rows(b), :]) * sqacc[rows(b), :]).astype(BF16)
            hm[GS, h, rows(b), :] = grad
            lifted = split(grad.astype(F32) * jnp.exp(colc[h, rows(b), :]), 1)
            both = dot(hm[QS, h, rows(b), :], lifted, 0, 0)
            parts.append(both[:, :HD] + both[:, HD:])
        g1[h] = parts[1]
        return (
            parts[0] + jnp.exp(end_row(h, 0)) * parts[1],
            jnp.exp(end_row(h, 0) + end_row(h, 1)),
        )

    begin(1, query_grad)

    def intra_backward(h, _):
        at_block = states(h)
        gain = gains[h, 0:1, :]
        for b in range(nblocks):
            ob[0, h, rows(b), :] = (att[h, rows(b), :] * sqacc[rows(b), :] * gain).astype(BF16)
            grad = hm[GS, h, rows(b), :]
            scores = (dot(grad, hm[VS, h, rows(b), :], 1, 1) * decay_table(h, b)).astype(BF16)
            carried = dot(twice(grad), split(at_block[b], 1), 1, 1)
            ob[1, h, rows(b), :] = (
                dot(scores, hm[KS, h, rows(b), :], 1, 0) + jnp.exp(colc[h, rows(b), :]) * carried
            ).astype(BF16)
            gkp[h, rows(b), :] = dot(scores, hm[QS, h, rows(b), :], 0, 0)
            gvp[h, rows(b), :] = dot(wts[h, b], grad, 0, 0)
        return 0

    lax.fori_loop(0, half, intra_backward, 0)
    middle(1)
    lax.fori_loop(half, heads, intra_backward, 0)
    store_rows(0, ob.at[0], normed_hbm)
    store_rows(1, ob.at[1], gq_hbm)

    def close(h):
        last = ee[1, h]
        at_block = (jnp.exp(end_row(h, 1)) * last + g1[h], last)
        for b in range(nblocks):
            scale = jnp.exp(end_row(h, b) - colc[h, rows(b), :])
            key = hm[KS, h, rows(b), :]
            value = hm[VS, h, rows(b), :]
            grad_k = gkp[h, rows(b), :] + scale * dot(twice(value), split(at_block[b], 1), 1, 1)
            grad_v = gvp[h, rows(b), :] + scale * dot(twice(key), split(at_block[b], 0), 1, 0)
            hm[KS, h, rows(b), :] = grad_k.astype(BF16)
            hm[VS, h, rows(b), :] = grad_v.astype(BF16)

    finish(1, close)
    store_rows(2, hm.at[KS], gk_hbm)
    store_rows(3, hm.at[VS], gv_hbm)
    drain(0)
    drain(1)
    for slot, dst in enumerate((normed_hbm, gq_hbm, gk_hbm, gv_hbm)):
        store_wait(slot, dst)


def on_device(chips, query_rows, key_rows, value_rows, output_grad, norm_gain, log_decay):
    tok, heads, _ = query_rows.shape
    half = heads // 2
    rows = jax.ShapeDtypeStruct((tok, heads, HD), BF16)
    hbm = pl.BlockSpec(memory_space=pl.ANY)
    vmem = pl.BlockSpec(memory_space=pltpu.VMEM)
    by_head = pltpu.VMEM((heads, tok, HD), F32)
    state = pltpu.VMEM((heads, HD, HD), F32)
    dma = pltpu.SemaphoreType.DMA
    return pl.pallas_call(
        functools.partial(kernel, chips),
        out_shape=(rows,) * 4,
        in_specs=[hbm] * 4 + [vmem] * 2,
        out_specs=[hbm] * 4,
        scratch_shapes=[
            pltpu.VMEM((4, tok, heads, HD), BF16),
            pltpu.VMEM((4, heads, tok, HD), BF16),
            pltpu.VMEM((heads, 8, tok), F32),
            by_head,
            by_head,
            pltpu.VMEM((heads, tok // BLOCK, BLOCK, BLOCK), BF16),
            by_head,
            by_head,
            state,
            state,
            pltpu.VMEM((2, heads, tok, HD), BF16),
            pltpu.VMEM((heads, 8, HD), F32),
            pltpu.VMEM((2, half, HD + PAD, HD), F32),
            pltpu.VMEM((2, half, HD + PAD, HD), F32),
            pltpu.VMEM((2, half, HD + PAD, HD), F32),
            pltpu.VMEM((2, chips, HD // 2 + PAD, HD), F32),
            pltpu.VMEM((2, chips, HD // 2 + PAD, HD), F32),
            pltpu.VMEM((2, chips, HD // 2, HD), F32),
            pltpu.VMEM((2, chips, HD // 2, HD), F32),
            pltpu.VMEM((2, half, HD, HD), F32),
            pltpu.VMEM((2, heads, HD, HD), F32),
            pltpu.VMEM((HEAD_TOTAL // heads, 8, tok), F32),
            pltpu.VMEM((tok, HD), F32),
            pltpu.VMEM((tok, HD), F32),
            dma((4,)),
            dma((4, tok // CHUNK)),
            dma((2, half)),
            dma((2, half)),
            dma((2, chips)),
            dma((2, chips)),
            dma((2, chips)),
            dma((2, chips)),
            dma((2, half)),
            dma((2, half)),
            dma((HEAD_TOTAL // heads,)),
            dma((HEAD_TOTAL // heads,)),
        ],
        compiler_params=pltpu.CompilerParams(
            collective_id=0, has_side_effects=True, vmem_limit_bytes=60 << 20
        ),
        cost_estimate=pl.CostEstimate(
            flops=2 * 10**10, bytes_accessed=16 << 20, transcendentals=10**7
        ),
    )(query_rows, key_rows, value_rows, output_grad, norm_gain, log_decay)


def solution(mesh):
    rows = P("seq", "head", None)
    return jax.shard_map(
        functools.partial(on_device, mesh.shape["seq"] // 2),
        mesh=mesh,
        in_specs=(rows, rows, rows, rows, P("head", None), P("head", "seq")),
        out_specs=(rows,) * 4,
        check_vma=False,
    )
```

profile of v0, /device:TPU:1, one launch (start us, length us, event | category | flops | bytes accessed | tf_op | source)
XLA Modules:
  0.0 80.7 jit_solution(7636566155215428411)
XLA Ops:
  0.6 70.6 %shard_map.93 = (bf16[512,16,128]{2,1,0:T(8,128)(2,1)}, bf16[512,16,128]{2,1,0:T(8,128)(2,1)}, bf16[512,16,128]{2,1,0:T(8,128)(2,1)}, bf16[512,16,128]{2,1,0:T(8,128)(2,1)}) custom-call(bf16[512,16,128]{2,1,0:T(8,128)(2,1)} %q_hbm.1, bf16[512,16,128]{2,1,0:T(8,128)(2,1)} %k_hbm.1, bf16[512,16,128]{2,1,0:T(8,128)(2,1)} %v_hbm.1, bf16[512,16,128]{2,1,0:T(8,128)(2,1)} %g_hbm.1, ...), custom_call_target="tpu_custom_call" | custom-call | flops 20000000000 | bytes 16777216 | tf_op jit(solution)/shard_map/pallas_call | solution.py:477
  71.3 0.0 copy-start.2
  71.3 3.4 %copy.14 = bf16[512,16,128]{2,1,0:T(8,128)(2,1)} copy(bf16[512,16,128]{2,1,0:T(8,128)(2,1)} %get-tuple-element.8) | data formatting | bytes 4194304
  74.7 0.0 copy-done.2
  74.7 0.0 copy-start.1
  74.7 1.3 %copy.15 = bf16[512,16,128]{2,1,0:T(8,128)(2,1)} copy(bf16[512,16,128]{2,1,0:T(8,128)(2,1)S(1)} %copy-done.2) | data formatting | bytes 4194304
  76.0 1.0 %copy-done.1 = bf16[512,16,128]{2,1,0:T(8,128)(2,1)S(1)} copy-done((bf16[512,16,128]{2,1,0:T(8,128)(2,1)S(1)}, bf16[512,16,128]{2,1,0:T(8,128)(2,1)}, u32[]{:S(2)}) %copy-start.1) | copy-done | bytes 2097176
  77.0 0.0 copy-start
  77.0 1.3 %copy.16 = bf16[512,16,128]{2,1,0:T(8,128)(2,1)} copy(bf16[512,16,128]{2,1,0:T(8,128)(2,1)S(1)} %copy-done.1) | data formatting | bytes 4194304
  78.4 1.0 %copy-done = bf16[512,16,128]{2,1,0:T(8,128)(2,1)S(1)} copy-done((bf16[512,16,128]{2,1,0:T(8,128)(2,1)S(1)}, bf16[512,16,128]{2,1,0:T(8,128)(2,1)}, u32[]{:S(2)}) %copy-start) | copy-done | bytes 2097176
  79.4 1.3 %copy.17 = bf16[512,16,128]{2,1,0:T(8,128)(2,1)} copy(bf16[512,16,128]{2,1,0:T(8,128)(2,1)S(1)} %copy-done) | data formatting | bytes 4194304
Async XLA Ops:
  71.3 3.4 %copy-start.2 = (bf16[512,16,128]{2,1,0:T(8,128)(2,1)S(1)}, bf16[512,16,128]{2,1,0:T(8,128)(2,1)}, u32[]{:S(2)}) copy-start(bf16[512,16,128]{2,1,0:T(8,128)(2,1)} %get-tuple-element.9) | copy-start | bytes 6291460
  74.7 2.3 %copy-start.1 = (bf16[512,16,128]{2,1,0:T(8,128)(2,1)S(1)}, bf16[512,16,128]{2,1,0:T(8,128)(2,1)}, u32[]{:S(2)}) copy-start(bf16[512,16,128]{2,1,0:T(8,128)(2,1)} %get-tuple-element.10) | copy-start | bytes 6291460
  77.0 2.3 %copy-start = (bf16[512,16,128]{2,1,0:T(8,128)(2,1)S(1)}, bf16[512,16,128]{2,1,0:T(8,128)(2,1)}, u32[]{:S(2)}) copy-start(bf16[512,16,128]{2,1,0:T(8,128)(2,1)} %get-tuple-element.11) | copy-start | bytes 6291460
where the time goes:
time: 81.2 us; the launch traced here: 80.7 us
  Pallas kernels  70.6 us (87%)
  local copies, waits for them, and re-layouts  9.43 us (12%)
    pallas_call x1, Pallas kernels, on_device(): pl.pallas_call(functools.partial(kernel, chips), out_shape=(rows,) * 4, i...  70.6 us
    unnamed x10, local copies, waits for them, and re-layouts  9.43 us

commit v1 on v0

v1 whole, which is shorter than its diff:
```python
import functools

import jax
import jax.numpy as jnp
from jax import lax
from jax.experimental import pallas as pl
from jax.experimental.pallas import tpu as pltpu
from jax.sharding import PartitionSpec as P

HEAD_TOTAL = 64
HD = 128
BLOCK = 256
CHUNK = 64
PAD = 8
FIRST_VMEM = 38 << 20
SECOND_VMEM = 14 << 20
MESH = pl.DeviceIdType.MESH
F32 = jnp.float32
BF16 = jnp.bfloat16


def dot(a, b, ca, cb):
    return lax.dot_general(a, b, (((ca,), (cb,)), ((), ())), preferred_element_type=F32)


def split(x, axis):
    hi = x.astype(BF16)
    lo = (x - hi.astype(F32)).astype(BF16)
    return jnp.concatenate([hi, lo], axis=axis)


def twice(x):
    return jnp.concatenate([x, x], axis=1)


def one_device_ids(chips):
    d = lax.axis_index("seq")
    c = d // 2
    return d, c, d - 2 * c


def block_rows(b):
    return slice(b * BLOCK, (b + 1) * BLOCK)


def close_heads(hs, state, gkp, gvp, colc, keys, values, put):
    tok = colc.shape[1]
    for b in range(tok // BLOCK):
        rows = block_rows(b)
        loaded = []
        for h in hs:
            gap = colc[h, tok - 1 : tok, :] - colc[h, rows, :]
            for later in range(b, tok // BLOCK - 1):
                gap = gap + colc[h, (later + 1) * BLOCK - 1 : (later + 1) * BLOCK, :]
            loaded.append(
                (jnp.exp(gap), keys[h, rows, :], values[h, rows, :], state[h], gkp[h, rows, :], gvp[h, rows, :])
            )
        done = []
        for scale, key, value, last, part_k, part_v in loaded:
            grad_k = part_k + scale * dot(twice(value), split(last, 1), 1, 1)
            grad_v = part_v + scale * dot(twice(key), split(last, 0), 1, 0)
            done.append((grad_k.astype(BF16), grad_v.astype(BF16)))
        for h, (grad_k, grad_v) in zip(hs, done):
            put(h, rows, grad_k, grad_v)


def first_kernel(
    chips,
    q_hbm,
    k_hbm,
    v_hbm,
    g_hbm,
    gain_ref,
    ld_ref,
    normed_t,
    gq_t,
    gk_h,
    gv_h,
    gkp,
    gvp,
    enter_b,
    colc,
    land,
    qs,
    gs,
    cumr,
    att,
    wts,
    s0,
    g0,
    g1,
    ob,
    gains,
    tx,
    tp,
    tm,
    sb,
    rb,
    pb,
    pin,
    es,
    enter_f,
    zb,
    sqacc,
    pracc,
    in_sem,
    p1s,
    p1r,
    a1s,
    a1r,
    a2s,
    a2r,
    p2s,
    p2r,
    zs,
    zr,
):
    heads, tok = ld_ref.shape
    half = heads // 2
    pairs = half // 2
    zcount = HEAD_TOTAL // heads
    z = lax.axis_index("head")
    d, c, core = one_device_ids(chips)
    partner = (2 * c + 1 - core, z)
    ks, vs = gk_h, gv_h
    enter = (enter_f, enter_b)

    def chip_dev(chip):
        return (2 * chip + core, z)

    sources = (k_hbm, v_hbm, q_hbm, g_hbm)
    by_heads = (ks, vs, qs, gs)

    def load(slot):
        return pltpu.make_async_copy(sources[slot], land.at[slot % 3], in_sem.at[slot])

    for slot in range(3):
        load(slot).start()

    barrier = pltpu.get_barrier_semaphore()

    def greet(i, _):
        pl.semaphore_signal(
            barrier, inc=1, device_id=chip_dev(lax.rem(c + i, chips)), device_id_type=MESH
        )
        return 0

    lax.fori_loop(1, chips, greet, 0)
    pl.semaphore_signal(barrier, inc=1, device_id=partner, device_id_type=MESH)
    for i in range(1, zcount):
        pl.semaphore_signal(
            barrier, inc=1, device_id=(d, lax.rem(z + i, zcount)), device_id_type=MESH
        )

    cum = ld_ref[...]
    lane = lax.broadcasted_iota(jnp.int32, cum.shape, 1) % BLOCK
    step = 1
    while step < BLOCK:
        cum = cum + jnp.where(lane >= step, pltpu.roll(cum, step, 1), 0.0)
        step *= 2
    for h in range(heads):
        cumr[h] = jnp.broadcast_to(cum[h : h + 1, :], (8, tok))
        gains[h] = jnp.broadcast_to(gain_ref[h : h + 1, :], (8, HD))

    def columns(h, _):
        colc[h] = jnp.transpose(jnp.broadcast_to(cumr[h, 0:1, :], (HD, tok)))
        return 0

    lax.fori_loop(0, heads, columns, 0)

    def to_heads(slot):
        load(slot).wait()

        def part(i, _):
            at = pl.ds(pl.multiple_of(i * CHUNK, CHUNK), CHUNK)
            by_heads[slot][:, at, :] = pltpu.einshape("thd->htd", land[slot % 3, at])
            return 0

        lax.fori_loop(0, tok // CHUNK, part, 0)

    def to_rows(src, dst):
        def part(i, _):
            at = pl.ds(pl.multiple_of(i * CHUNK, CHUNK), CHUNK)
            dst[at] = pltpu.einshape("htd->thd", src[:, at, :])
            return 0

        lax.fori_loop(0, tok // CHUNK, part, 0)

    def end_row(h, b):
        return colc[h, (b + 1) * BLOCK - 1 : (b + 1) * BLOCK, :]

    mask = lax.broadcasted_iota(jnp.int32, (BLOCK, BLOCK), 0) >= lax.broadcasted_iota(
        jnp.int32, (BLOCK, BLOCK), 1
    )

    def decay_table(h, b):
        gap = twice(colc[h, block_rows(b), :]) - cumr[h, 0:1, block_rows(b)]
        return jnp.exp(jnp.where(mask, gap, -jnp.inf))

    def pair1(w, j):
        return pltpu.make_async_remote_copy(
            tx.at[w, j],
            tp.at[w, j],
            p1s.at[w, j],
            p1r.at[w, j],
            device_id=partner,
            device_id_type=MESH,
        )

    def spread1(w, dest, src):
        return pltpu.make_async_remote_copy(
            sb.at[w, dest],
            rb.at[w, src],
            a1s.at[w, dest],
            a1r.at[w, src],
            device_id=chip_dev(dest),
            device_id_type=MESH,
        )

    def spread2(w, dest, src):
        return pltpu.make_async_remote_copy(
            pb.at[w, dest],
            pin.at[w, src],
            a2s.at[w, dest],
            a2r.at[w, src],
            device_id=chip_dev(dest),
            device_id_type=MESH,
        )

    def pair2(w, j, owner):
        return pltpu.make_async_remote_copy(
            es.at[w, j],
            enter[w].at[owner * half + j],
            p2s.at[w, j],
            p2r.at[w, j],
            device_id=partner,
            device_id_type=MESH,
        )

    def far_first(i):
        return lax.rem(c + 1 + lax.rem(i + 5, chips - 1), chips)

    def begin(w, local_totals):
        first = (core == 0) if w == 0 else (core == 1)

        def theirs(i, _):
            js = (2 * i, 2 * i + 1)
            for j, (total, decay) in zip(js, local_totals([(1 - core) * half + j for j in js])):
                tx[w, j, :HD] = total
                tx[w, j, HD:] = jnp.broadcast_to(decay, (PAD, HD))
                pair1(w, j).start()
            return 0

        lax.fori_loop(0, pairs, theirs, 0)

        def ours(i, _):
            pair = lax.rem(i + c // 4 + pairs // 2, pairs)
            js = (2 * pair, 2 * pair + 1)
            for j, (total, decay) in zip(js, local_totals([core * half + j for j in js])):
                tm[w, j, :HD] = total
                tm[w, j, HD:] = jnp.broadcast_to(decay, (PAD, HD))
                pair1(w, j).wait_recv()
                other = tp[w, j, :HD]
                other_decay = tp[w, j, HD : HD + 1]
                chip_total = (
                    jnp.where(first, other_decay, 1.0) * total + jnp.where(first, 1.0, decay) * other
                )
                chip_decay = jnp.broadcast_to(decay * other_decay, (PAD, HD))
                for part in range(2):
                    dest = 2 * j + part
                    piece = chip_total[part * (HD // 2) : (part + 1) * (HD // 2)]
                    sb[w, dest, : HD // 2] = piece
                    sb[w, dest, HD // 2 :] = chip_decay

                    @pl.when(dest != c)
                    def _():
                        spread1(w, dest, c).start()

            return 0

        lax.fori_loop(0, pairs, ours, 0)
        rb[w, c] = sb[w, c]

    def middle(w):
        def wait(i, _):
            src = lax.rem(c + i, chips)
            spread1(w, src, src).wait_recv()
            return 0

        lax.fori_loop(1, chips, wait, 0)
        carried = jnp.zeros((HD // 2, HD), F32)
        for i in range(chips):
            src = i if w == 0 else chips - 1 - i
            pb[w, src] = carried
            carried = rb[w, src, HD // 2 : HD // 2 + 1] * carried + rb[w, src, : HD // 2]

        def send(i, _):
            spread2(w, far_first(i), c).start()
            return 0

        lax.fori_loop(0, chips - 1, send, 0)
        pin[w, c] = pb[w, c]

    def finish(w):
        first = (core == 0) if w == 0 else (core == 1)

        def ours(i, _):
            j = lax.rem(i + c // 2, half)
            for part in range(2):
                src = 2 * j + part

                @pl.when(src != c)
                def _():
                    spread2(w, src, src).wait_recv()

            entering = jnp.concatenate([pin[w, 2 * j], pin[w, 2 * j + 1]], axis=0)
            decay = jnp.where(first, tm[w, j, HD : HD + 1], tp[w, j, HD : HD + 1])
            total = jnp.where(first, tm[w, j, :HD], tp[w, j, :HD])
            after = decay * entering + total
            es[w, j] = jnp.where(first, after, entering)
            pair2(w, j, core).start()
            enter[w][core * half + j] = jnp.where(first, entering, after)
            return 0

        lax.fori_loop(0, half, ours, 0)

    def drain(w):
        def by_pair(j, _):
            pair1(w, j).wait_send()
            pair2(w, j, core).wait_send()
            return 0

        lax.fori_loop(0, half, by_pair, 0)

        def spreads(i, _):
            dest = lax.rem(c + i, chips)
            spread1(w, dest, c).wait_send()
            spread2(w, dest, c).wait_send()
            return 0

        lax.fori_loop(1, chips, spreads, 0)

    to_heads(0)
    load(3).start()
    to_heads(1)

    def key_value(hs):
        loaded = [
            [
                (
                    ks[h, block_rows(b), :],
                    vs[h, block_rows(b), :].astype(F32),
                    jnp.exp(end_row(h, b) - colc[h, block_rows(b), :]),
                )
                for b in range(2)
            ]
            for h in hs
        ]
        ends = [(jnp.exp(end_row(h, 0)), jnp.exp(end_row(h, 1))) for h in hs]
        out = []
        for h, blocks, (end0, end1) in zip(hs, loaded, ends):
            parts = []
            for key, value, scale in blocks:
                both = dot(key, split(value * scale, 1), 0, 0)
                parts.append(both[:, :HD] + both[:, HD:])
            out.append((end1 * parts[0] + parts[1], end0 * end1, parts[0]))
        for h, (_, _, part) in zip(hs, out):
            s0[h] = part
        return [o[:2] for o in out]

    pl.semaphore_wait(barrier, chips - 1 + 1 + zcount - 1)
    begin(0, key_value)
    to_heads(2)

    def intra_forward(h, _):
        for b in range(2):
            rows = block_rows(b)
            query = qs[h, rows, :]
            raw = dot(query, ks[h, rows, :], 1, 1)
            weights = (raw * decay_table(h, b)).astype(BF16)
            wts[h, b] = weights
            inner = dot(weights, vs[h, rows, :], 1, 0)
            if b == 1:
                inner = inner + jnp.exp(colc[h, rows, :]) * dot(twice(query), split(s0[h], 0), 1, 0)
            att[h, rows, :] = inner
        return 0

    lax.fori_loop(0, half, intra_forward, 0)
    middle(0)
    lax.fori_loop(half, heads, intra_forward, 0)
    to_heads(3)
    sqacc[...] = jnp.zeros_like(sqacc)
    pracc[...] = jnp.zeros_like(pracc)

    def attend(hs, b):
        rows = block_rows(b)
        loaded = []
        for h in hs:
            gap = colc[h, rows, :] if b == 0 else colc[h, rows, :] + end_row(h, 0)
            loaded.append(
                (
                    qs[h, rows, :],
                    enter_f[h],
                    jnp.exp(gap),
                    att[h, rows, :],
                    gains[h, 0:1, :] * gs[h, rows, :].astype(F32),
                )
            )
        squares, products = sqacc[rows, :], pracc[rows, :]
        done = []
        for query, state, scale, inner, scaled in loaded:
            whole = inner + scale * dot(twice(query), split(state, 0), 1, 0)
            squares += whole * whole
            products += scaled * whole
            done.append(whole)
        for h, whole in zip(hs, done):
            att[h, rows, :] = whole
        sqacc[rows, :] = squares
        pracc[rows, :] = products

    def across(b, i):
        return pltpu.make_async_remote_copy(
            zb.at[b, 0],
            zb.at[b, i],
            zs.at[b, i],
            zr.at[b, i],
            device_id=(d, lax.rem(z + i, zcount)),
            device_id_type=MESH,
        )

    finish(0)
    for b in range(2):

        def attend_ours(i, _):
            attend([core * half + 2 * i, core * half + 2 * i + 1], b)
            return 0

        def attend_theirs(i, _):
            pair = lax.rem(i + c // 4, pairs)
            js = (2 * pair, 2 * pair + 1)
            if b == 0:
                for j in js:
                    pair2(0, j, 1 - core).wait_recv()
            attend([(1 - core) * half + j for j in js], b)
            return 0

        lax.fori_loop(0, pairs, attend_ours, 0)
        lax.fori_loop(0, pairs, attend_theirs, 0)
        rows = block_rows(b)
        zb[b, 0, 0:1, :] = jnp.sum(jnp.transpose(sqacc[rows, :]), axis=0, keepdims=True)
        zb[b, 0, 1:2, :] = jnp.sum(jnp.transpose(pracc[rows, :]), axis=0, keepdims=True)
        zb[b, 0, 2:, :] = jnp.zeros((6, BLOCK), F32)
        for i in range(1, zcount):
            across(b, i).start()

    def grads(hs, b):
        rows = block_rows(b)
        loaded = [
            (
                gains[h, 0:1, :] * gs[h, rows, :].astype(F32),
                att[h, rows, :],
                jnp.exp(colc[h, rows, :]),
                qs[h, rows, :],
            )
            for h in hs
        ]
        inv, shift = sqacc[rows, :], pracc[rows, :]
        out = []
        for scaled, whole, scale, query in loaded:
            grad = ((scaled - whole * shift) * inv).astype(BF16)
            both = dot(query, split(grad.astype(F32) * scale, 1), 0, 0)
            out.append((grad, both[:, :HD] + both[:, HD:]))
        for h, (grad, _) in zip(hs, out):
            gs[h, rows, :] = grad
        return [part for _, part in out]

    def norms(b):
        for i in range(1, zcount):
            across(b, i).wait()
        summed = zb[b, 0]
        for i in range(1, zcount):
            summed = summed + zb[b, i]
        inv_row = lax.rsqrt(summed[0:1, :] / (HEAD_TOTAL * HD) + 1e-06)
        mean_row = summed[1:2, :] * inv_row / (HEAD_TOTAL * HD)
        rows = block_rows(b)
        sqacc[rows, :] = jnp.transpose(jnp.broadcast_to(inv_row, (HD, BLOCK)))
        pracc[rows, :] = jnp.transpose(jnp.broadcast_to(inv_row * mean_row, (HD, BLOCK)))

    norms(0)

    def early_grads(i, _):
        hs = (2 * i, 2 * i + 1)
        for h, part in zip(hs, grads(hs, 0)):
            g0[h] = part
        return 0

    lax.fori_loop(0, heads // 2, early_grads, 0)
    norms(1)

    def late_grads(hs):
        early = [(g0[h], jnp.exp(end_row(h, 0)), jnp.exp(end_row(h, 1))) for h in hs]
        parts = grads(hs, 1)
        for h, part in zip(hs, parts):
            g1[h] = part
        return [(part0 + end0 * part1, end0 * end1) for (part0, end0, end1), part1 in zip(early, parts)]

    begin(1, late_grads)

    def intra_backward(h, _):
        enter_h = enter_f[h]
        at_block = (enter_h, jnp.exp(end_row(h, 0)) * enter_h + s0[h])
        gain = gains[h, 0:1, :]
        for b in range(2):
            rows = block_rows(b)
            ob[0, h, rows, :] = (att[h, rows, :] * sqacc[rows, :] * gain).astype(BF16)
            grad = gs[h, rows, :]
            key, value = ks[h, rows, :], vs[h, rows, :]
            scores = (dot(grad, value, 1, 1) * decay_table(h, b)).astype(BF16)
            carried = dot(twice(grad), split(at_block[b], 1), 1, 1)
            ob[1, h, rows, :] = (
                dot(scores, key, 1, 0) + jnp.exp(colc[h, rows, :]) * carried
            ).astype(BF16)
            part_k = dot(scores, qs[h, rows, :], 0, 0)
            part_v = dot(wts[h, b], grad, 0, 0)
            if b == 0:
                scale = jnp.exp(end_row(h, 0) - colc[h, rows, :])
                part_k = part_k + scale * dot(twice(value), split(g1[h], 1), 1, 1)
                part_v = part_v + scale * dot(twice(key), split(g1[h], 0), 1, 0)
            gkp[h, rows, :] = part_k
            gvp[h, rows, :] = part_v
        return 0

    lax.fori_loop(0, half, intra_backward, 0)
    middle(1)
    lax.fori_loop(half, heads, intra_backward, 0)
    to_rows(ob.at[0], normed_t)
    to_rows(ob.at[1], gq_t)
    finish(1)

    def put(h, rows, grad_k, grad_v):
        gk_h[h, rows, :] = grad_k
        gv_h[h, rows, :] = grad_v

    def close_ours(i, _):
        hs = [core * half + 2 * i, core * half + 2 * i + 1]
        close_heads(hs, enter_b, gkp, gvp, colc, ks, vs, put)
        return 0

    lax.fori_loop(0, pairs, close_ours, 0)

    def arrived(j, _):
        pair2(1, j, 1 - core).wait_recv()
        return 0

    lax.fori_loop(0, half, arrived, 0)
    drain(0)
    drain(1)


def second_kernel(
    normed_t,
    gq_t,
    gk_h,
    gv_h,
    gkp,
    gvp,
    enter_b,
    colc,
    normed_hbm,
    gq_hbm,
    gk_hbm,
    gv_hbm,
    done_k,
    done_v,
    land,
    first_sem,
    out_sem,
):
    heads, tok = colc.shape[0], colc.shape[1]
    half = heads // 2
    core = lax.rem(lax.axis_index("seq"), 2)
    ready = [
        pltpu.make_async_copy(src, dst, first_sem.at[i])
        for i, (src, dst) in enumerate(((normed_t, normed_hbm), (gq_t, gq_hbm)))
    ]
    for copy in ready:
        copy.start()

    def put(h, rows, grad_k, grad_v):
        done_k[h, rows, :] = grad_k
        done_v[h, rows, :] = grad_v

    def close_theirs(i, _):
        hs = [(1 - core) * half + 2 * i, (1 - core) * half + 2 * i + 1]
        close_heads(hs, enter_b, gkp, gvp, colc, gk_h, gv_h, put)
        for j in range(2):
            h = core * half + 2 * i + j
            done_k[h] = gk_h[h]
            done_v[h] = gv_h[h]
        return 0

    lax.fori_loop(0, half // 2, close_theirs, 0)
    outs = ((done_k, gk_hbm), (done_v, gv_hbm))

    def out(slot, i):
        at = pl.ds(pl.multiple_of(i * CHUNK, CHUNK), CHUNK)
        return pltpu.make_async_copy(land.at[slot, at], outs[slot][1].at[at], out_sem.at[slot, i])

    for slot in range(2):

        def part(i, _):
            at = pl.ds(pl.multiple_of(i * CHUNK, CHUNK), CHUNK)
            land[slot, at] = pltpu.einshape("htd->thd", outs[slot][0][:, at, :])
            out(slot, i).start()
            return 0

        lax.fori_loop(0, tok // CHUNK, part, 0)
    for slot in range(2):

        def wait(i, _):
            out(slot, i).wait()
            return 0

        lax.fori_loop(0, tok // CHUNK, wait, 0)
    for copy in ready:
        copy.wait()


def on_device(chips, query_rows, key_rows, value_rows, output_grad, norm_gain, log_decay):
    tok, heads, _ = query_rows.shape
    half = heads // 2
    zcount = HEAD_TOTAL // heads
    rows = jax.ShapeDtypeStruct((tok, heads, HD), BF16)
    hbm = pl.BlockSpec(memory_space=pl.ANY)
    vmem = pl.BlockSpec(memory_space=pltpu.VMEM)
    dma = pltpu.SemaphoreType.DMA

    def by_head(dtype):
        return pltpu.VMEM((heads, tok, HD), dtype)

    state = pltpu.VMEM((heads, HD, HD), F32)
    between = (
        pltpu.VMEM((tok, heads, HD), BF16),
        pltpu.VMEM((tok, heads, HD), BF16),
        by_head(BF16),
        by_head(BF16),
        by_head(F32),
        by_head(F32),
        state,
        by_head(F32),
    )
    made = pl.pallas_call(
        functools.partial(first_kernel, chips),
        out_shape=between,
        in_specs=[hbm] * 4 + [vmem] * 2,
        out_specs=[vmem] * len(between),
        scratch_shapes=[
            pltpu.VMEM((3, tok, heads, HD), BF16),
            by_head(BF16),
            by_head(BF16),
            pltpu.VMEM((heads, 8, tok), F32),
            by_head(F32),
            pltpu.VMEM((heads, tok // BLOCK, BLOCK, BLOCK), BF16),
            state,
            state,
            state,
            pltpu.VMEM((2, heads, tok, HD), BF16),
            pltpu.VMEM((heads, 8, HD), F32),
            pltpu.VMEM((2, half, HD + PAD, HD), F32),
            pltpu.VMEM((2, half, HD + PAD, HD), F32),
            pltpu.VMEM((2, half, HD + PAD, HD), F32),
            pltpu.VMEM((2, chips, HD // 2 + PAD, HD), F32),
            pltpu.VMEM((2, chips, HD // 2 + PAD, HD), F32),
            pltpu.VMEM((2, chips, HD // 2, HD), F32),
            pltpu.VMEM((2, chips, HD // 2, HD), F32),
            pltpu.VMEM((2, half, HD, HD), F32),
            state,
            pltpu.VMEM((2, zcount, 8, BLOCK), F32),
            pltpu.VMEM((tok, HD), F32),
            pltpu.VMEM((tok, HD), F32),
            dma((4,)),
            dma((2, half)),
            dma((2, half)),
            dma((2, chips)),
            dma((2, chips)),
            dma((2, chips)),
            dma((2, chips)),
            dma((2, half)),
            dma((2, half)),
            dma((2, zcount)),
            dma((2, zcount)),
        ],
        compiler_params=pltpu.CompilerParams(
            collective_id=0, has_side_effects=True, vmem_limit_bytes=FIRST_VMEM
        ),
        cost_estimate=pl.CostEstimate(
            flops=2 * 10**10, bytes_accessed=8 << 20, transcendentals=10**7
        ),
    )(query_rows, key_rows, value_rows, output_grad, norm_gain, log_decay)
    made = [pltpu.with_memory_space_constraint(m, pltpu.VMEM) for m in made]
    return pl.pallas_call(
        second_kernel,
        out_shape=(rows,) * 4,
        in_specs=[vmem] * len(between),
        out_specs=[hbm] * 4,
        scratch_shapes=[
            by_head(BF16),
            by_head(BF16),
            pltpu.VMEM((2, tok, heads, HD), BF16),
            dma((2,)),
            dma((2, tok // CHUNK)),
        ],
        compiler_params=pltpu.CompilerParams(vmem_limit_bytes=SECOND_VMEM),
        cost_estimate=pl.CostEstimate(
            flops=2 * 10**9, bytes_accessed=8 << 20, transcendentals=10**6
        ),
    )(*made)


def solution(mesh):
    rows = P("seq", "head", None)
    return jax.shard_map(
        functools.partial(on_device, mesh.shape["seq"] // 2),
        mesh=mesh,
        in_specs=(rows, rows, rows, rows, P("head", None), P("head", "seq")),
        out_specs=(rows,) * 4,
        check_vma=False,
    )
```

time: 81.2 us -> 71.2 us (0.88)
  local copies, waits for them, and re-layouts: 9.43 us -> 0 us
    unnamed x10 -> x0, local copies, waits for them, and re-layouts: 9.43 us -> none
    pallas_call x1 -> x2, Pallas kernels: 70.6 us -> 70.3 us  [the longest x1 66.2 us: on_device(): pl.pallas_call(functools.partial(first_kernel, chips), out_shape=between,...]
where the time goes in v1:
time: 71.2 us; the launch traced here: 71 us
  Pallas kernels  70.3 us (99%)
    pallas_call x1, Pallas kernels, on_device(): pl.pallas_call(functools.partial(first_kernel, chips), out_shape=between,...  66.2 us
    pallas_call x1, Pallas kernels, on_device(): pl.pallas_call(second_kernel, out_shape=(rows,) * 4, in_specs=[vmem] * le...  4.14 us

profile of v1, /device:TPU:1, one launch (start us, length us, event | category | flops | bytes accessed | tf_op | source)
XLA Modules:
  0.0 71.0 jit_solution(8416121397733531339)
XLA Ops:
  0.6 66.2 %shard_map.93 = (bf16[512,16,128]{2,1,0:T(8,128)(2,1)S(1)}, bf16[512,16,128]{2,1,0:T(8,128)(2,1)S(1)}, bf16[16,512,128]{2,1,0:T(8,128)(2,1)S(1)}, bf16[16,512,12...) custom-call(bf16[512,16,128]{2,1,0:T(8,128)(2,1)} %q_hbm.1, ...), custom_call_target="tpu_custom_call" | custom-call | flops 20000000000 | bytes 8388608 | tf_op jit(solution)/shard_map/pallas_call | solution.py:652
  66.8 4.1 %shard_map.94 = (bf16[512,16,128]{2,1,0:T(8,128)(2,1)}, bf16[512,16,128]{2,1,0:T(8,128)(2,1)}, bf16[512,16,128]{2,1,0:T(8,128)(2,1)}, bf16[512,16,128]{2,1,0:T(8,128)(2,1)}) custom-call(bf16[512,16,128]{2,1,0:T(8,128)(2,1)S(1)} %get-tuple-element.12.normed_t, bf16[512,16,128]{2,1,0:T(8,128)(2,1)S(1)} %get-tuple-element.13.gq_t, ...), custom_call_target="tpu_custom_call" | custom-call | flops 2000000000 | bytes 8388608 | tf_op jit(solution)/shard_map/pallas_call | solution.py:701

commit v2 on v1

--- a/solution.py
+++ b/solution.py
@@ -12,6 +12,7 @@
 BLOCK = 256
 CHUNK = 64
 PAD = 8
+EARLY = 6
 FIRST_VMEM = 38 << 20
 SECOND_VMEM = 14 << 20
 MESH = pl.DeviceIdType.MESH
@@ -29,6 +30,22 @@
     return jnp.concatenate([hi, lo], axis=axis)
 
 
+def split3(x):
+    hi = x.astype(BF16).astype(F32)
+    mid = (x - hi).astype(BF16).astype(F32)
+    lo = (x - hi - mid).astype(BF16).astype(F32)
+    return jnp.concatenate([hi, mid, lo], axis=0)
+
+
+def far_offsets(chips):
+    side = int(chips**0.5)
+
+    def hops(o):
+        return sum(min(n, side - n) for n in divmod(o, side))
+
+    return sorted(range(1, chips), key=lambda o: (-hops(o), o))
+
+
 def twice(x):
     return jnp.concatenate([x, x], axis=1)
 
@@ -43,17 +60,14 @@
     return slice(b * BLOCK, (b + 1) * BLOCK)
 
 
-def close_heads(hs, state, gkp, gvp, colc, keys, values, put):
-    tok = colc.shape[1]
-    for b in range(tok // BLOCK):
+def close_heads(hs, state, gkp, gvp, kcol, decs, keys, values, put):
+    for b in range(2):
         rows = block_rows(b)
         loaded = []
         for h in hs:
-            gap = colc[h, tok - 1 : tok, :] - colc[h, rows, :]
-            for later in range(b, tok // BLOCK - 1):
-                gap = gap + colc[h, (later + 1) * BLOCK - 1 : (later + 1) * BLOCK, :]
+            last = state[h] * decs[1, h, 0:1, :] if b == 0 else state[h]
             loaded.append(
-                (jnp.exp(gap), keys[h, rows, :], values[h, rows, :], state[h], gkp[h, rows, :], gvp[h, rows, :])
+                (kcol[h, rows, :], keys[h, rows, :], values[h, rows, :], last, gkp[h, rows, :], gvp[h, rows, :])
             )
         done = []
         for scale, key, value, last, part_k, part_v in loaded:
@@ -79,17 +93,19 @@
     gkp,
     gvp,
     enter_b,
-    colc,
+    kcol,
+    decs,
     land,
     qs,
     gs,
     cumr,
+    colc,
+    ecol,
     att,
     wts,
     s0,
     g0,
     g1,
-    ob,
     gains,
     tx,
     tp,
@@ -132,62 +148,71 @@
     by_heads = (ks, vs, qs, gs)
 
     def load(slot):
-        return pltpu.make_async_copy(sources[slot], land.at[slot % 3], in_sem.at[slot])
-
-    for slot in range(3):
+        return pltpu.make_async_copy(sources[slot], land.at[slot % 2], in_sem.at[slot])
+
+    for slot in range(2):
         load(slot).start()
-
     barrier = pltpu.get_barrier_semaphore()
-
-    def greet(i, _):
+    offsets = far_offsets(chips)
+    for o in offsets:
         pl.semaphore_signal(
-            barrier, inc=1, device_id=chip_dev(lax.rem(c + i, chips)), device_id_type=MESH
+            barrier, inc=1, device_id=chip_dev(lax.rem(c + o, chips)), device_id_type=MESH
         )
-        return 0
-
-    lax.fori_loop(1, chips, greet, 0)
-    pl.semaphore_signal(barrier, inc=1, device_id=partner, device_id_type=MESH)
     for i in range(1, zcount):
         pl.semaphore_signal(
             barrier, inc=1, device_id=(d, lax.rem(z + i, zcount)), device_id_type=MESH
         )
-
-    cum = ld_ref[...]
-    lane = lax.broadcasted_iota(jnp.int32, cum.shape, 1) % BLOCK
-    step = 1
-    while step < BLOCK:
-        cum = cum + jnp.where(lane >= step, pltpu.roll(cum, step, 1), 0.0)
-        step *= 2
+    pl.semaphore_signal(barrier, inc=1, device_id=partner, device_id_type=MESH)
+
+    triangle = (
+        lax.broadcasted_iota(jnp.int32, (BLOCK, BLOCK), 0)
+        <= lax.broadcasted_iota(jnp.int32, (BLOCK, BLOCK), 1)
+    ).astype(BF16)
+    terms = split3(ld_ref[...]).astype(BF16)
+    cums = []
+    for b in range(2):
+        summed = dot(terms[:, block_rows(b)], triangle, 1, 0)
+        cums.append(summed[:heads] + summed[heads : 2 * heads] + summed[2 * heads :])
+    ends = [cum[:, BLOCK - 1 :] for cum in cums]
+    for b in range(2):
+        decay = jnp.broadcast_to(jnp.exp(ends[b]), (heads, HD))
+        for h in range(heads):
+            decs[b, h] = jnp.broadcast_to(decay[h : h + 1, :], (8, HD))
     for h in range(heads):
-        cumr[h] = jnp.broadcast_to(cum[h : h + 1, :], (8, tok))
         gains[h] = jnp.broadcast_to(gain_ref[h : h + 1, :], (8, HD))
 
-    def columns(h, _):
-        colc[h] = jnp.transpose(jnp.broadcast_to(cumr[h, 0:1, :], (HD, tok)))
-        return 0
-
-    lax.fori_loop(0, heads, columns, 0)
+    def columns(x, out):
+        padded = jnp.concatenate([split3(x), jnp.zeros((HD - 3 * heads, tok), F32)], axis=0)
+        upright = jnp.transpose(padded).astype(BF16)
+        term_head = lax.broadcasted_iota(jnp.int32, (HD, 2 * HD), 0) % heads
+        lane_head = lax.broadcasted_iota(jnp.int32, (HD, 2 * HD), 1) // HD
+
+        for i in range(heads // 2):
+            pick = (term_head == lane_head + 2 * i).astype(F32).astype(BF16)
+            both = dot(upright, pick, 1, 0)
+            out[2 * i] = both[:, :HD]
+            out[2 * i + 1] = both[:, HD:]
+
+    cum = jnp.concatenate(cums, axis=1)
+    columns(jnp.concatenate([jnp.exp(e - x) for e, x in zip(ends, cums)], axis=1), kcol)
 
     def to_heads(slot):
         load(slot).wait()
 
         def part(i, _):
             at = pl.ds(pl.multiple_of(i * CHUNK, CHUNK), CHUNK)
-            by_heads[slot][:, at, :] = pltpu.einshape("thd->htd", land[slot % 3, at])
+            by_heads[slot][:, at, :] = pltpu.einshape("thd->htd", land[slot % 2, at])
             return 0
 
         lax.fori_loop(0, tok // CHUNK, part, 0)
 
-    def to_rows(src, dst):
+    def to_rows(get, dst):
         def part(i, _):
             at = pl.ds(pl.multiple_of(i * CHUNK, CHUNK), CHUNK)
-            dst[at] = pltpu.einshape("htd->thd", src[:, at, :])
+            dst[at] = pltpu.einshape("htd->thd", get(at))
             return 0
 
         lax.fori_loop(0, tok // CHUNK, part, 0)
-
-    def end_row(h, b):
-        return colc[h, (b + 1) * BLOCK - 1 : (b + 1) * BLOCK, :]
 
     mask = lax.broadcasted_iota(jnp.int32, (BLOCK, BLOCK), 0) >= lax.broadcasted_iota(
         jnp.int32, (BLOCK, BLOCK), 1
@@ -199,7 +224,7 @@
 
     def pair1(w, j):
         return pltpu.make_async_remote_copy(
-            tx.at[w, j],
+            tx.at[j],
             tp.at[w, j],
             p1s.at[w, j],
             p1r.at[w, j],
@@ -209,7 +234,7 @@
 
     def spread1(w, dest, src):
         return pltpu.make_async_remote_copy(
-            sb.at[w, dest],
+            sb.at[dest],
             rb.at[w, src],
             a1s.at[w, dest],
             a1r.at[w, src],
@@ -219,7 +244,7 @@
 
     def spread2(w, dest, src):
         return pltpu.make_async_remote_copy(
-            pb.at[w, dest],
+            pb.at[dest],
             pin.at[w, src],
             a2s.at[w, dest],
             a2r.at[w, src],
@@ -229,7 +254,7 @@
 
     def pair2(w, j, owner):
         return pltpu.make_async_remote_copy(
-            es.at[w, j],
+            es.at[j],
             enter[w].at[owner * half + j],
             p2s.at[w, j],
             p2r.at[w, j],
@@ -237,69 +262,69 @@
             device_id_type=MESH,
         )
 
-    def far_first(i):
-        return lax.rem(c + 1 + lax.rem(i + 5, chips - 1), chips)
-
     def begin(w, local_totals):
         first = (core == 0) if w == 0 else (core == 1)
 
-        def theirs(i, _):
-            js = (2 * i, 2 * i + 1)
-            for j, (total, decay) in zip(js, local_totals([(1 - core) * half + j for j in js])):
-                tx[w, j, :HD] = total
-                tx[w, j, HD:] = jnp.broadcast_to(decay, (PAD, HD))
-                pair1(w, j).start()
-            return 0
-
-        lax.fori_loop(0, pairs, theirs, 0)
-
-        def ours(i, _):
+        def one(s, _):
+            is_ours = jnp.logical_or(s == 2 * pairs - 1, jnp.logical_and(s >= 2, s % 2 == 0))
+            i = jnp.where(is_ours, jnp.where(s == 2 * pairs - 1, pairs - 1, s // 2 - 1), (s + 1) // 2)
             pair = lax.rem(i + c // 4 + pairs // 2, pairs)
             js = (2 * pair, 2 * pair + 1)
-            for j, (total, decay) in zip(js, local_totals([core * half + j for j in js])):
-                tm[w, j, :HD] = total
-                tm[w, j, HD:] = jnp.broadcast_to(decay, (PAD, HD))
-                pair1(w, j).wait_recv()
-                other = tp[w, j, :HD]
-                other_decay = tp[w, j, HD : HD + 1]
-                chip_total = (
-                    jnp.where(first, other_decay, 1.0) * total + jnp.where(first, 1.0, decay) * other
-                )
-                chip_decay = jnp.broadcast_to(decay * other_decay, (PAD, HD))
-                for part in range(2):
-                    dest = 2 * j + part
-                    piece = chip_total[part * (HD // 2) : (part + 1) * (HD // 2)]
-                    sb[w, dest, : HD // 2] = piece
-                    sb[w, dest, HD // 2 :] = chip_decay
-
-                    @pl.when(dest != c)
-                    def _():
-                        spread1(w, dest, c).start()
-
-            return 0
-
-        lax.fori_loop(0, pairs, ours, 0)
-        rb[w, c] = sb[w, c]
+            base = jnp.where(is_ours, core, 1 - core) * half
+            totals = local_totals([base + j for j in js])
+            if w == 0:
+
+                @pl.when(s == 0)
+                def _():
+                    pl.semaphore_wait(barrier, chips - 1 + 1 + zcount - 1)
+
+            @pl.when(jnp.logical_not(is_ours))
+            def _():
+                for j, (total, decay) in zip(js, totals):
+                    tx[j, :HD] = total
+                    tx[j, HD:] = jnp.broadcast_to(decay, (PAD, HD))
+                    pair1(w, j).start()
+
+            @pl.when(is_ours)
+            def _():
+                for j, (total, decay) in zip(js, totals):
+                    tm[j, :HD] = total
+                    tm[j, HD:] = jnp.broadcast_to(decay, (PAD, HD))
+                    pair1(w, j).wait_recv()
+                    other = tp[w, j, :HD]
+                    other_decay = tp[w, j, HD : HD + 1]
+                    chip_total = (
+                        jnp.where(first, other_decay, 1.0) * total
+                        + jnp.where(first, 1.0, decay) * other
+                    )
+                    chip_decay = jnp.broadcast_to(decay * other_decay, (PAD, HD))
+                    for part in range(2):
+                        dest = 2 * j + part
+                        sb[dest, : HD // 2] = chip_total[part * (HD // 2) : (part + 1) * (HD // 2)]
+                        sb[dest, HD // 2 :] = chip_decay
+
+                        @pl.when(dest != c)
+                        def _():
+                            spread1(w, dest, c).start()
+
+            return 0
+
+        lax.fori_loop(0, 2 * pairs, one, 0)
+        rb[w, c] = sb[c]
 
     def middle(w):
-        def wait(i, _):
-            src = lax.rem(c + i, chips)
+        for o in reversed(offsets):
+            src = lax.rem(c + o, chips)
             spread1(w, src, src).wait_recv()
-            return 0
-
-        lax.fori_loop(1, chips, wait, 0)
         carried = jnp.zeros((HD // 2, HD), F32)
         for i in range(chips):
             src = i if w == 0 else chips - 1 - i
-            pb[w, src] = carried
+            pb[src] = carried
             carried = rb[w, src, HD // 2 : HD // 2 + 1] * carried + rb[w, src, : HD // 2]
 
-        def send(i, _):
-            spread2(w, far_first(i), c).start()
-            return 0
-
-        lax.fori_loop(0, chips - 1, send, 0)
-        pin[w, c] = pb[w, c]
+        for o in offsets:
+            spread2(w, lax.rem(c + o, chips), c).start()
+        pin[w, c] = pb[c]
 
     def finish(w):
         first = (core == 0) if w == 0 else (core == 1)
@@ -314,10 +339,10 @@
                     spread2(w, src, src).wait_recv()
 
             entering = jnp.concatenate([pin[w, 2 * j], pin[w, 2 * j + 1]], axis=0)
-            decay = jnp.where(first, tm[w, j, HD : HD + 1], tp[w, j, HD : HD + 1])
-            total = jnp.where(first, tm[w, j, :HD], tp[w, j, :HD])
+            decay = jnp.where(first, tm[j, HD : HD + 1], tp[w, j, HD : HD + 1])
+            total = jnp.where(first, tm[j, :HD], tp[w, j, :HD])
             after = decay * entering + total
-            es[w, j] = jnp.where(first, after, entering)
+            es[j] = jnp.where(first, after, entering)
             pair2(w, j, core).start()
             enter[w][core * half + j] = jnp.where(first, entering, after)
             return 0
@@ -341,24 +366,21 @@
         lax.fori_loop(1, chips, spreads, 0)
 
     to_heads(0)
+    load(2).start()
+    to_heads(1)
     load(3).start()
-    to_heads(1)
 
     def key_value(hs):
         loaded = [
             [
-                (
-                    ks[h, block_rows(b), :],
-                    vs[h, block_rows(b), :].astype(F32),
-                    jnp.exp(end_row(h, b) - colc[h, block_rows(b), :]),
-                )
+                (ks[h, block_rows(b), :], vs[h, block_rows(b), :].astype(F32), kcol[h, block_rows(b), :])
                 for b in range(2)
             ]
             for h in hs
         ]
-        ends = [(jnp.exp(end_row(h, 0)), jnp.exp(end_row(h, 1))) for h in hs]
+        decays = [(decs[0, h, 0:1, :], decs[1, h, 0:1, :]) for h in hs]
         out = []
-        for h, blocks, (end0, end1) in zip(hs, loaded, ends):
+        for blocks, (end0, end1) in zip(loaded, decays):
             parts = []
             for key, value, scale in blocks:
                 both = dot(key, split(value * scale, 1), 0, 0)
@@ -368,8 +390,11 @@
             s0[h] = part
         return [o[:2] for o in out]
 
-    pl.semaphore_wait(barrier, chips - 1 + 1 + zcount - 1)
     begin(0, key_value)
+    for h in range(heads):
+        cumr[h] = jnp.broadcast_to(cum[h : h + 1, :], (8, tok))
+    columns(cum, colc)
+    columns(jnp.exp(cum), ecol)
     to_heads(2)
 
     def intra_forward(h, _):
@@ -381,13 +406,13 @@
             wts[h, b] = weights
             inner = dot(weights, vs[h, rows, :], 1, 0)
             if b == 1:
-                inner = inner + jnp.exp(colc[h, rows, :]) * dot(twice(query), split(s0[h], 0), 1, 0)
+                inner = inner + ecol[h, rows, :] * dot(twice(query), split(s0[h], 0), 1, 0)
             att[h, rows, :] = inner
         return 0
 
-    lax.fori_loop(0, half, intra_forward, 0)
+    lax.fori_loop(0, EARLY, intra_forward, 0)
     middle(0)
-    lax.fori_loop(half, heads, intra_forward, 0)
+    lax.fori_loop(EARLY, heads, intra_forward, 0)
     to_heads(3)
     sqacc[...] = jnp.zeros_like(sqacc)
     pracc[...] = jnp.zeros_like(pracc)
@@ -396,12 +421,12 @@
         rows = block_rows(b)
         loaded = []
         for h in hs:
-            gap = colc[h, rows, :] if b == 0 else colc[h, rows, :] + end_row(h, 0)
+            state = enter_f[h] if b == 0 else enter_f[h] * decs[0, h, 0:1, :]
             loaded.append(
                 (
                     qs[h, rows, :],
-                    enter_f[h],
-                    jnp.exp(gap),
+                    state,
+                    ecol[h, rows, :],
                     att[h, rows, :],
                     gains[h, 0:1, :] * gs[h, rows, :].astype(F32),
                 )
@@ -432,20 +457,19 @@
     for b in range(2):
 
         def attend_ours(i, _):
-            attend([core * half + 2 * i, core * half + 2 * i + 1], b)
+            attend([core * half + 4 * i + n for n in range(4)], b)
             return 0
 
         def attend_theirs(i, _):
-            pair = lax.rem(i + c // 4, pairs)
-            js = (2 * pair, 2 * pair + 1)
+            js = [4 * i + n for n in range(4)]
             if b == 0:
                 for j in js:
                     pair2(0, j, 1 - core).wait_recv()
             attend([(1 - core) * half + j for j in js], b)
             return 0
 
-        lax.fori_loop(0, pairs, attend_ours, 0)
-        lax.fori_loop(0, pairs, attend_theirs, 0)
+        lax.fori_loop(0, pairs // 2, attend_ours, 0)
+        lax.fori_loop(0, pairs // 2, attend_theirs, 0)
         rows = block_rows(b)
         zb[b, 0, 0:1, :] = jnp.sum(jnp.transpose(sqacc[rows, :]), axis=0, keepdims=True)
         zb[b, 0, 1:2, :] = jnp.sum(jnp.transpose(pracc[rows, :]), axis=0, keepdims=True)
@@ -459,7 +483,7 @@
             (
                 gains[h, 0:1, :] * gs[h, rows, :].astype(F32),
                 att[h, rows, :],
-                jnp.exp(colc[h, rows, :]),
+                ecol[h, rows, :],
                 qs[h, rows, :],
             )
             for h in hs
@@ -489,41 +513,39 @@
     norms(0)
 
     def early_grads(i, _):
-        hs = (2 * i, 2 * i + 1)
+        hs = [4 * i + n for n in range(4)]
         for h, part in zip(hs, grads(hs, 0)):
             g0[h] = part
         return 0
 
-    lax.fori_loop(0, heads // 2, early_grads, 0)
+    lax.fori_loop(0, heads // 4, early_grads, 0)
     norms(1)
 
     def late_grads(hs):
-        early = [(g0[h], jnp.exp(end_row(h, 0)), jnp.exp(end_row(h, 1))) for h in hs]
+        early = [(g0[h], decs[0, h, 0:1, :], decs[1, h, 0:1, :]) for h in hs]
         parts = grads(hs, 1)
         for h, part in zip(hs, parts):
             g1[h] = part
         return [(part0 + end0 * part1, end0 * end1) for (part0, end0, end1), part1 in zip(early, parts)]
 
+    drain(0)
     begin(1, late_grads)
 
     def intra_backward(h, _):
         enter_h = enter_f[h]
-        at_block = (enter_h, jnp.exp(end_row(h, 0)) * enter_h + s0[h])
-        gain = gains[h, 0:1, :]
+        at_block = (enter_h, decs[0, h, 0:1, :] * enter_h + s0[h])
         for b in range(2):
             rows = block_rows(b)
-            ob[0, h, rows, :] = (att[h, rows, :] * sqacc[rows, :] * gain).astype(BF16)
             grad = gs[h, rows, :]
             key, value = ks[h, rows, :], vs[h, rows, :]
             scores = (dot(grad, value, 1, 1) * decay_table(h, b)).astype(BF16)
             carried = dot(twice(grad), split(at_block[b], 1), 1, 1)
-            ob[1, h, rows, :] = (
-                dot(scores, key, 1, 0) + jnp.exp(colc[h, rows, :]) * carried
-            ).astype(BF16)
+            grad_q = dot(scores, key, 1, 0) + ecol[h, rows, :] * carried
             part_k = dot(scores, qs[h, rows, :], 0, 0)
+            qs[h, rows, :] = grad_q.astype(BF16)
             part_v = dot(wts[h, b], grad, 0, 0)
             if b == 0:
-                scale = jnp.exp(end_row(h, 0) - colc[h, rows, :])
+                scale = kcol[h, rows, :]
                 part_k = part_k + scale * dot(twice(value), split(g1[h], 1), 1, 1)
                 part_v = part_v + scale * dot(twice(key), split(g1[h], 0), 1, 0)
             gkp[h, rows, :] = part_k
@@ -533,8 +555,13 @@
     lax.fori_loop(0, half, intra_backward, 0)
     middle(1)
     lax.fori_loop(half, heads, intra_backward, 0)
-    to_rows(ob.at[0], normed_t)
-    to_rows(ob.at[1], gq_t)
+
+    def normed_part(at):
+        gain = jnp.concatenate([gains[h, 0:1, :] for h in range(heads)], axis=0)
+        return (att[:, at, :] * sqacc[at, :][None] * gain[:, None, :]).astype(BF16)
+
+    to_rows(normed_part, normed_t)
+    to_rows(lambda at: qs[:, at, :], gq_t)
     finish(1)
 
     def put(h, rows, grad_k, grad_v):
@@ -543,7 +570,7 @@
 
     def close_ours(i, _):
         hs = [core * half + 2 * i, core * half + 2 * i + 1]
-        close_heads(hs, enter_b, gkp, gvp, colc, ks, vs, put)
+        close_heads(hs, enter_b, gkp, gvp, kcol, decs, ks, vs, put)
         return 0
 
     lax.fori_loop(0, pairs, close_ours, 0)
@@ -553,7 +580,6 @@
         return 0
 
     lax.fori_loop(0, half, arrived, 0)
-    drain(0)
     drain(1)
 
 
@@ -565,7 +591,8 @@
     gkp,
     gvp,
     enter_b,
-    colc,
+    kcol,
+    decs,
     normed_hbm,
     gq_hbm,
     gk_hbm,
@@ -576,7 +603,7 @@
     first_sem,
     out_sem,
 ):
-    heads, tok = colc.shape[0], colc.shape[1]
+    heads, tok = kcol.shape[0], kcol.shape[1]
     half = heads // 2
     core = lax.rem(lax.axis_index("seq"), 2)
     ready = [
@@ -592,7 +619,7 @@
 
     def close_theirs(i, _):
         hs = [(1 - core) * half + 2 * i, (1 - core) * half + 2 * i + 1]
-        close_heads(hs, enter_b, gkp, gvp, colc, gk_h, gv_h, put)
+        close_heads(hs, enter_b, gkp, gvp, kcol, decs, gk_h, gv_h, put)
         for j in range(2):
             h = core * half + 2 * i + j
             done_k[h] = gk_h[h]
@@ -648,6 +675,7 @@
         by_head(F32),
         state,
         by_head(F32),
+        pltpu.VMEM((2, heads, 8, HD), F32),
     )
     made = pl.pallas_call(
         functools.partial(first_kernel, chips),
@@ -655,25 +683,26 @@
         in_specs=[hbm] * 4 + [vmem] * 2,
         out_specs=[vmem] * len(between),
         scratch_shapes=[
-            pltpu.VMEM((3, tok, heads, HD), BF16),
+            pltpu.VMEM((2, tok, heads, HD), BF16),
             by_head(BF16),
             by_head(BF16),
             pltpu.VMEM((heads, 8, tok), F32),
+            by_head(F32),
+            by_head(F32),
             by_head(F32),
             pltpu.VMEM((heads, tok // BLOCK, BLOCK, BLOCK), BF16),
             state,
             state,
             state,
-            pltpu.VMEM((2, heads, tok, HD), BF16),
             pltpu.VMEM((heads, 8, HD), F32),
+            pltpu.VMEM((half, HD + PAD, HD), F32),
             pltpu.VMEM((2, half, HD + PAD, HD), F32),
-            pltpu.VMEM((2, half, HD + PAD, HD), F32),
-            pltpu.VMEM((2, half, HD + PAD, HD), F32),
+            pltpu.VMEM((half, HD + PAD, HD), F32),
+            pltpu.VMEM((chips, HD // 2 + PAD, HD), F32),
             pltpu.VMEM((2, chips, HD // 2 + PAD, HD), F32),
-            pltpu.VMEM((2, chips, HD // 2 + PAD, HD), F32),
+            pltpu.VMEM((chips, HD // 2, HD), F32),
             pltpu.VMEM((2, chips, HD // 2, HD), F32),
-            pltpu.VMEM((2, chips, HD // 2, HD), F32),
-            pltpu.VMEM((2, half, HD, HD), F32),
+            pltpu.VMEM((half, HD, HD), F32),
             state,
             pltpu.VMEM((2, zcount, 8, BLOCK), F32),
             pltpu.VMEM((tok, HD), F32),

time: 71.2 us -> 66.7 us (0.937)
  Pallas kernels: 70.3 us -> 65.9 us
    pallas_call x1, Pallas kernels: 66.2 us -> 61.7 us  [on_device(): pl.pallas_call(functools.partial(first_kernel, chips), out_shape=between,...]
where the time goes in v2:
time: 66.7 us; the launch traced here: 66.5 us
  Pallas kernels  65.9 us (99%)
    pallas_call x1, Pallas kernels, on_device(): pl.pallas_call(functools.partial(first_kernel, chips), out_shape=between,...  61.7 us
    pallas_call x1, Pallas kernels, on_device(): pl.pallas_call(second_kernel, out_shape=(rows,) * 4, in_specs=[vmem] * le...  4.15 us

profile of v2, /device:TPU:1, one launch (start us, length us, event | category | flops | bytes accessed | tf_op | source)
XLA Modules:
  0.0 66.5 jit_solution(17718295032591340236)
XLA Ops:
  0.6 61.7 %shard_map.93 = (bf16[512,16,128]{2,1,0:T(8,128)(2,1)S(1)}, bf16[512,16,128]{2,1,0:T(8,128)(2,1)S(1)}, bf16[16,512,128]{2,1,0:T(8,128)(2,1)S(1)}, bf16[16,512,12...) custom-call(bf16[512,16,128]{2,1,0:T(8,128)(2,1)} %q_hbm.1, ...), custom_call_target="tpu_custom_call" | custom-call | flops 20000000000 | bytes 8388608 | tf_op jit(solution)/shard_map/pallas_call | solution.py:680
  62.4 4.1 %shard_map.94 = (bf16[512,16,128]{2,1,0:T(8,128)(2,1)}, bf16[512,16,128]{2,1,0:T(8,128)(2,1)}, bf16[512,16,128]{2,1,0:T(8,128)(2,1)}, bf16[512,16,128]{2,1,0:T(8,128)(2,1)}) custom-call(bf16[512,16,128]{2,1,0:T(8,128)(2,1)S(1)} %get-tuple-element.13.normed_t, bf16[512,16,128]{2,1,0:T(8,128)(2,1)S(1)} %get-tuple-element.14.gq_t, ...), custom_call_target="tpu_custom_call" | custom-call | flops 2000000000 | bytes 8388608 | tf_op jit(solution)/shard_map/pallas_call | solution.py:730

commit v3 on v2

--- a/solution.py
+++ b/solution.py
@@ -224,8 +224,8 @@
 
     def pair1(w, j):
         return pltpu.make_async_remote_copy(
-            tx.at[j],
-            tp.at[w, j],
+            tx.at[j] if w == 0 else tx.at[j, :HD],
+            tp.at[w, j] if w == 0 else tp.at[w, j, :HD],
             p1s.at[w, j],
             p1r.at[w, j],
             device_id=partner,
@@ -234,8 +234,8 @@
 
     def spread1(w, dest, src):
         return pltpu.make_async_remote_copy(
-            sb.at[dest],
-            rb.at[w, src],
+            sb.at[dest] if w == 0 else sb.at[dest, : HD // 2],
+            rb.at[w, src] if w == 0 else rb.at[w, src, : HD // 2],
             a1s.at[w, dest],
             a1r.at[w, src],
             device_id=chip_dev(dest),
@@ -266,10 +266,10 @@
         first = (core == 0) if w == 0 else (core == 1)
 
         def one(s, _):
-            is_ours = jnp.logical_or(s == 2 * pairs - 1, jnp.logical_and(s >= 2, s % 2 == 0))
-            i = jnp.where(is_ours, jnp.where(s == 2 * pairs - 1, pairs - 1, s // 2 - 1), (s + 1) // 2)
-            pair = lax.rem(i + c // 4 + pairs // 2, pairs)
-            js = (2 * pair, 2 * pair + 1)
+            is_ours = s >= pairs // 2
+            i = jnp.where(is_ours, s - pairs // 2, s)
+            group = lax.rem(i + c // 8 + 1, pairs // 2)
+            js = [4 * group + n for n in range(4)]
             base = jnp.where(is_ours, core, 1 - core) * half
             totals = local_totals([base + j for j in js])
             if w == 0:
@@ -282,17 +282,19 @@
             def _():
                 for j, (total, decay) in zip(js, totals):
                     tx[j, :HD] = total
-                    tx[j, HD:] = jnp.broadcast_to(decay, (PAD, HD))
+                    if w == 0:
+                        tx[j, HD:] = jnp.broadcast_to(decay, (PAD, HD))
                     pair1(w, j).start()
 
             @pl.when(is_ours)
             def _():
                 for j, (total, decay) in zip(js, totals):
                     tm[j, :HD] = total
-                    tm[j, HD:] = jnp.broadcast_to(decay, (PAD, HD))
+                    if w == 0:
+                        tm[j, HD:] = jnp.broadcast_to(decay, (PAD, HD))
                     pair1(w, j).wait_recv()
                     other = tp[w, j, :HD]
-                    other_decay = tp[w, j, HD : HD + 1]
+                    other_decay = tp[0, j, HD : HD + 1]
                     chip_total = (
                         jnp.where(first, other_decay, 1.0) * total
                         + jnp.where(first, 1.0, decay) * other
@@ -301,16 +303,22 @@
                     for part in range(2):
                         dest = 2 * j + part
                         sb[dest, : HD // 2] = chip_total[part * (HD // 2) : (part + 1) * (HD // 2)]
-                        sb[dest, HD // 2 :] = chip_decay
-
-                        @pl.when(dest != c)
-                        def _():
-                            spread1(w, dest, c).start()
-
-            return 0
-
-        lax.fori_loop(0, 2 * pairs, one, 0)
-        rb[w, c] = sb[c]
+                        if w == 0:
+                            sb[dest, HD // 2 :] = chip_decay
+                for o in (2, 6, 1, 3, 5, 7, 4, 0):
+                    dest = len(js) * 2 * group + lax.rem(c + o, len(js) * 2)
+
+                    @pl.when(dest != c)
+                    def _():
+                        spread1(w, dest, c).start()
+
+            return 0
+
+        lax.fori_loop(0, pairs, one, 0)
+        if w == 0:
+            rb[w, c] = sb[c]
+        else:
+            rb[w, c, : HD // 2] = sb[c, : HD // 2]
 
     def middle(w):
         for o in reversed(offsets):
@@ -320,7 +328,7 @@
         for i in range(chips):
             src = i if w == 0 else chips - 1 - i
             pb[src] = carried
-            carried = rb[w, src, HD // 2 : HD // 2 + 1] * carried + rb[w, src, : HD // 2]
+            carried = rb[0, src, HD // 2 : HD // 2 + 1] * carried + rb[w, src, : HD // 2]
 
         for o in offsets:
             spread2(w, lax.rem(c + o, chips), c).start()
@@ -339,7 +347,7 @@
                     spread2(w, src, src).wait_recv()
 
             entering = jnp.concatenate([pin[w, 2 * j], pin[w, 2 * j + 1]], axis=0)
-            decay = jnp.where(first, tm[j, HD : HD + 1], tp[w, j, HD : HD + 1])
+            decay = jnp.where(first, tm[j, HD : HD + 1], tp[0, j, HD : HD + 1])
             total = jnp.where(first, tm[j, :HD], tp[w, j, :HD])
             after = decay * entering + total
             es[j] = jnp.where(first, after, entering)
@@ -569,11 +577,11 @@
         gv_h[h, rows, :] = grad_v
 
     def close_ours(i, _):
-        hs = [core * half + 2 * i, core * half + 2 * i + 1]
+        hs = [core * half + 4 * i + n for n in range(4)]
         close_heads(hs, enter_b, gkp, gvp, kcol, decs, ks, vs, put)
         return 0
 
-    lax.fori_loop(0, pairs, close_ours, 0)
+    lax.fori_loop(0, pairs // 2, close_ours, 0)
 
     def arrived(j, _):
         pair2(1, j, 1 - core).wait_recv()
@@ -618,15 +626,15 @@
         done_v[h, rows, :] = grad_v
 
     def close_theirs(i, _):
-        hs = [(1 - core) * half + 2 * i, (1 - core) * half + 2 * i + 1]
+        hs = [(1 - core) * half + 4 * i + n for n in range(4)]
         close_heads(hs, enter_b, gkp, gvp, kcol, decs, gk_h, gv_h, put)
-        for j in range(2):
-            h = core * half + 2 * i + j
+        for j in range(4):
+            h = core * half + 4 * i + j
             done_k[h] = gk_h[h]
             done_v[h] = gv_h[h]
         return 0
 
-    lax.fori_loop(0, half // 2, close_theirs, 0)
+    lax.fori_loop(0, half // 4, close_theirs, 0)
     outs = ((done_k, gk_hbm), (done_v, gv_hbm))
 
     def out(slot, i):

time: 66.7 us -> 63 us (0.945)
  Pallas kernels: 65.9 us -> 62.2 us
    pallas_call x1, Pallas kernels: 61.7 us -> 58.3 us  [on_device(): pl.pallas_call(functools.partial(first_kernel, chips), out_shape=between,...]
where the time goes in v3:
time: 63 us; the launch traced here: 62.8 us
  Pallas kernels  62.2 us (99%)
  between operations  0.64 us (1%)
    pallas_call x1, Pallas kernels, on_device(): pl.pallas_call(functools.partial(first_kernel, chips), out_shape=between,...  58.3 us
    pallas_call x1, Pallas kernels, on_device(): pl.pallas_call(second_kernel, out_shape=(rows,) * 4, in_specs=[vmem] * le...  3.89 us

profile of v3, /device:TPU:1, one launch (start us, length us, event | category | flops | bytes accessed | tf_op | source)
XLA Modules:
  0.0 62.8 jit_solution(9005075806435091282)
XLA Ops:
  0.6 58.3 %shard_map.93 = (bf16[512,16,128]{2,1,0:T(8,128)(2,1)S(1)}, bf16[512,16,128]{2,1,0:T(8,128)(2,1)S(1)}, bf16[16,512,128]{2,1,0:T(8,128)(2,1)S(1)}, bf16[16,512,12...) custom-call(bf16[512,16,128]{2,1,0:T(8,128)(2,1)} %q_hbm.1, ...), custom_call_target="tpu_custom_call" | custom-call | flops 20000000000 | bytes 8388608 | tf_op jit(solution)/shard_map/pallas_call | solution.py:688
  58.9 3.9 %shard_map.94 = (bf16[512,16,128]{2,1,0:T(8,128)(2,1)}, bf16[512,16,128]{2,1,0:T(8,128)(2,1)}, bf16[512,16,128]{2,1,0:T(8,128)(2,1)}, bf16[512,16,128]{2,1,0:T(8,128)(2,1)}) custom-call(bf16[512,16,128]{2,1,0:T(8,128)(2,1)S(1)} %get-tuple-element.13.normed_t, bf16[512,16,128]{2,1,0:T(8,128)(2,1)S(1)} %get-tuple-element.14.gq_t, ...), custom_call_target="tpu_custom_call" | custom-call | flops 2000000000 | bytes 8388608 | tf_op jit(solution)/shard_map/pallas_call | solution.py:738

commit v4 on v3

--- a/solution.py
+++ b/solution.py
@@ -305,8 +305,9 @@
                         sb[dest, : HD // 2] = chip_total[part * (HD // 2) : (part + 1) * (HD // 2)]
                         if w == 0:
                             sb[dest, HD // 2 :] = chip_decay
-                for o in (2, 6, 1, 3, 5, 7, 4, 0):
-                    dest = len(js) * 2 * group + lax.rem(c + o, len(js) * 2)
+                for fx, fy in ((0, 2), (0, 1), (0, 3), (1, 2), (0, 0), (1, 1), (1, 3), (1, 0)):
+                    column = lax.rem(c // 4 + fx + i, 2)
+                    dest = len(js) * 2 * group + 4 * column + lax.rem(c + fy, 4)
 
                     @pl.when(dest != c)
                     def _():

time: 63 us -> 63 us (level)
  no operation moved by 1% of the time
where the time goes in v4:
time: 63 us; the launch traced here: 62.8 us
  Pallas kernels  62.2 us (99%)
  between operations  0.64 us (1%)
    pallas_call x1, Pallas kernels, on_device(): pl.pallas_call(functools.partial(first_kernel, chips), out_shape=between,...  58.3 us
    pallas_call x1, Pallas kernels, on_device(): pl.pallas_call(second_kernel, out_shape=(rows,) * 4, in_specs=[vmem] * le...  3.89 us

profile of v4, /device:TPU:1, one launch (start us, length us, event | category | flops | bytes accessed | tf_op | source)
XLA Modules:
  0.0 62.8 jit_solution(15509042168413777354)
XLA Ops:
  0.6 58.3 %shard_map.93 = (bf16[512,16,128]{2,1,0:T(8,128)(2,1)S(1)}, bf16[512,16,128]{2,1,0:T(8,128)(2,1)S(1)}, bf16[16,512,128]{2,1,0:T(8,128)(2,1)S(1)}, bf16[16,512,12...) custom-call(bf16[512,16,128]{2,1,0:T(8,128)(2,1)} %q_hbm.1, ...), custom_call_target="tpu_custom_call" | custom-call | flops 20000000000 | bytes 8388608 | tf_op jit(solution)/shard_map/pallas_call | solution.py:689
  58.9 3.9 %shard_map.94 = (bf16[512,16,128]{2,1,0:T(8,128)(2,1)}, bf16[512,16,128]{2,1,0:T(8,128)(2,1)}, bf16[512,16,128]{2,1,0:T(8,128)(2,1)}, bf16[512,16,128]{2,1,0:T(8,128)(2,1)}) custom-call(bf16[512,16,128]{2,1,0:T(8,128)(2,1)S(1)} %get-tuple-element.13.normed_t, bf16[512,16,128]{2,1,0:T(8,128)(2,1)S(1)} %get-tuple-element.14.gq_t, ...), custom_call_target="tpu_custom_call" | custom-call | flops 2000000000 | bytes 8388608 | tf_op jit(solution)/shard_map/pallas_call | solution.py:739
